TPU v7x, 32 devices: a whole 2x2x4 slice. The times are simulated.
32 devices in a mesh: group: 1, expert: 32 (over z, y, x, core).
Axes of the slice: x: 2, y: 2, z: 4, core: 2. Of those that a mesh axis runs over, the one named last changes fastest.
Arguments:
- tokens: bfloat16 [256, 2880], P(('group', 'expert')), may hold values from -6 to 6
- routes: int32 [256, 4], P(('group', 'expert')), may hold values from 0 to 7, all different within a row; in each aligned block of 8 rows (0 to 7, 8 to 15, ...) at most 8 rows name the same one
- gates: bfloat16 [256, 4], P(('group', 'expert')), may hold values from 0.099609375 to 1
- w_gate: bfloat16 [32, 2880, 360], P('expert'), may hold values from -0.109375 to 0.109375
- w_up: bfloat16 [32, 2880, 360], P('expert'), may hold values from -0.109375 to 0.109375
- w_down: bfloat16 [32, 360, 2880], P('expert'), may hold values from -0.15625 to 0.15625
- w_enc: bfloat16 [2880, 16384], P(None, 'expert'), may hold values from -0.109375 to 0.109375
- b_enc: float32 [16384], P('expert'), may hold values from -1 to 0.25
- w_dec: bfloat16 [16384, 2880], P('expert'), may hold values from -0.046875 to 0.046875
- b_dec: float32 [2880], replicated, may hold values from -3 to 3
Outputs:
- residual: bfloat16 [256, 2880], P(('group', 'expert'))
Inputs may be any that keep to these rules, and one draw needn't show every extreme that they name: `routes`: each row names 4 different experts. Among the rows of one device no expert is named by more than 8 rows, a bound that some block reaches.
All inputs are finite; a program needn't handle non-finite values.
Results may differ from a plain program's by a relative error of at most 0.0048.
Values may be sent and summed in bfloat16 or wider, within the bound.
A program may use at most 128 MiB of HBM per device.

v0:
```python
import jax
import jax.numpy as jnp
from jax import lax
from jax.sharding import PartitionSpec as P

SLABS = 4


def source_layout(routes, gates, experts, capacity):
    tok_dev, topk = routes.shape
    pairs = tok_dev * topk
    flat_routes = routes.reshape(pairs)
    one_hot = (flat_routes[:, None] == jnp.arange(experts, dtype=jnp.int32)[None, :]).astype(
        jnp.int32
    )
    rank_in = jnp.sum((jnp.cumsum(one_hot, axis=0) - 1) * one_hot, axis=1)
    target = flat_routes * capacity + rank_in
    pair_token = jnp.arange(pairs, dtype=jnp.int32) // topk
    slot_token = jnp.full((experts * capacity,), tok_dev, jnp.int32).at[target].set(pair_token)
    slot_gate = jnp.zeros((experts * capacity,), gates.dtype).at[target].set(gates.reshape(pairs))
    return (slot_token, slot_gate)


def widen(array, experts, copies):
    capacity = array.shape[0] // experts
    shaped = array.reshape((experts, capacity) + array.shape[1:])
    spread = jnp.repeat(shaped, copies, axis=0)
    return spread.reshape((experts * copies * capacity,) + array.shape[1:])


def shards(tokens, routes, gates, w_gate, w_up, w_down, w_enc, b_enc, w_dec, b_dec):
    tok_dev, topk = routes.shape
    devices = lax.axis_size("expert")
    experts = devices // SLABS
    capacity = min(tok_dev, 2 * tok_dev * topk // experts)
    features = jnp.maximum(
        jnp.dot(
            lax.all_gather(tokens, "expert", axis=0, tiled=True),
            w_enc,
            preferred_element_type=jnp.float32,
        )
        + b_enc,
        0.0,
    ).astype(jnp.bfloat16)
    slot_token, slot_gate = source_layout(routes, gates, experts, capacity)
    send_rows = jnp.take(tokens, slot_token, axis=0, mode="fill", fill_value=0)
    expert_rows, expert_gate, local_token = (
        lax.all_to_all(
            widen(send_rows, experts, SLABS), "expert", split_axis=0, concat_axis=0, tiled=True
        ),
        lax.all_to_all(
            widen(slot_gate, experts, SLABS), "expert", split_axis=0, concat_axis=0, tiled=True
        ),
        lax.all_to_all(
            widen(slot_token, experts, SLABS), "expert", split_axis=0, concat_axis=0, tiled=True
        ),
    )
    gate_pre = jnp.dot(expert_rows, w_gate[0], preferred_element_type=jnp.float32)
    up_pre = jnp.dot(expert_rows, w_up[0], preferred_element_type=jnp.float32)
    hidden = ((up_pre + 1.0) * gate_pre * jax.nn.sigmoid(1.702 * gate_pre)).astype(jnp.bfloat16)
    partial_out = jnp.dot(hidden, w_down[0], preferred_element_type=jnp.float32)
    weighted = partial_out * expert_gate.astype(jnp.float32)[:, None]
    returned = lax.all_to_all(weighted, "expert", split_axis=0, concat_axis=0, tiled=True)
    own_token, unused_gate = source_layout(routes, gates, experts, capacity)
    back_token = widen(own_token, experts, SLABS)
    layer_out = (
        jnp.zeros((tok_dev, tokens.shape[1]), jnp.float32).at[back_token].add(returned, mode="drop")
    )
    prediction = lax.psum_scatter(
        jnp.dot(features, w_dec, preferred_element_type=jnp.float32),
        "expert",
        scatter_dimension=0,
        tiled=True,
    )
    return (layer_out - prediction - b_dec).astype(jnp.bfloat16)


def solution(mesh):
    in_specs = (
        P(("group", "expert"), None),
        P(("group", "expert"), None),
        P(("group", "expert"), None),
        P("expert", None, None),
        P("expert", None, None),
        P("expert", None, None),
        P(None, "expert"),
        P("expert"),
        P("expert", None),
        P(),
    )
    out_specs = P(("group", "expert"), None)
    return jax.shard_map(shards, mesh=mesh, in_specs=in_specs, out_specs=out_specs, check_vma=False)
```

profile of v0, /device:TPU:0, one launch (start us, length us, event | category | flops | bytes accessed | tf_op | source)
XLA Modules:
  0.0 302.6 jit_solution(6801326867101963245)
XLA Ops:
  6.5 0.0 copy-start
  6.5 0.0 copy-start.1
  6.5 0.9 copy.24
  7.5 0.7 broadcast_multiply_fusion
  8.2 0.1 eq.8
  8.2 0.1 fusion.48
  8.3 0.1 reduce_window_sum.12
  8.4 0.2 select_reduce_fusion
  8.6 0.1 copy.23
  8.6 0.1 mul.39
  8.7 0.8 copy.25
  9.5 0.1 reshape.121
  9.6 0.8 scatter_custom_fusion.1
  10.4 0.1 reshape.99
  10.5 0.6 copy.26
  11.1 7.3 %all-to-all-start.1 = ((bf16[32,8,1]{1,2,0:T(2,128)(2,1)}), bf16[32,8,1]{1,2,0:T(2,128)(2,1)S(1)}, u32[]{:S(2)}, u32[]{:S(2)}) async-start(bf16[32,8,1]{1,2,0:T(2,128)(2,1)} %copy.26), calls=%async_computation.1 | async-start | bytes 32768 | tf_op jit(solution)/shard_map/all_to_all | solution.py:51
  18.4 0.7 scatter_custom_fusion
  19.1 0.1 broadcast_in_dim.40
  19.2 0.0 copy-done.1
  19.2 1.5 gather_fusion
  20.7 1.1 bitcast_select_fusion
  21.8 3.6 %all-to-all-done.1 = bf16[32,8,1]{1,2,0:T(2,128)(2,1)S(1)} async-done(((bf16[32,8,1]{1,2,0:T(2,128)(2,1)}), bf16[32,8,1]{1,2,0:T(2,128)(2,1)S(1)}, u32[]{:S(2)}, u32[]{:S(2)}) %all-to-all-start.1) | async-done | bytes 544 | tf_op jit(solution)/shard_map/all_to_all | solution.py:51
  25.5 1.2 broadcast_in_dim.44
  26.7 3.4 %all-to-all-start = ((bf16[32,8,2880]{2,1,0:T(8,128)(2,1)}), bf16[32,8,2880]{2,1,0:T(8,128)(2,1)}, u32[]{:S(2)}, u32[]{:S(2)}) async-start(bf16[32,8,2880]{2,1,0:T(8,128)(2,1)} %bitcast.53), calls=%async_computation | async-start | bytes 3014656 | tf_op jit(solution)/shard_map/all_to_all | solution.py:48
  30.1 0.1 convert_reduce_fusion
  30.2 0.1 reshape.100
  30.2 36.3 %all-to-all-done = bf16[32,8,2880]{2,1,0:T(8,128)(2,1)} async-done(((bf16[32,8,2880]{2,1,0:T(8,128)(2,1)}), bf16[32,8,2880]{2,1,0:T(8,128)(2,1)}, u32[]{:S(2)}, u32[]{:S(2)}) %all-to-all-start) | async-done | bytes 1474592 | tf_op jit(solution)/shard_map/all_to_all | solution.py:48
  66.6 2.8 fusion.3
  69.4 7.1 %convolution_multiply_fusion = f32[256,2880]{0,1:T(8,128)} fusion(bf16[1,360,2880]{2,1,0:T(8,128)(2,1)} %param.15, f32[256]{0:T(256)S(1)} %reshape.100, f32[256,360]{0,1:T(8,128)S(1)} %fusion.3, bf16[1,2880,360]{1,2,0:T(8,128)(2,1)} %param.14, bf16[32,8,2880]{2,1,0:T(8,128)(2,1)} %all-to-all-done), kind=kOutput, calls=%fused_computation.4 | convolution fusion | flops 1063157760 | bytes 8940544 | tf_op jit(solution)/shard_map/dot_general | solution.py:61
  76.5 3.5 %copy.27 = f32[256,2880]{1,0:T(8,128)} copy(f32[256,2880]{0,1:T(8,128)} %convolution_multiply_fusion) | data formatting | bytes 5898240 | tf_op jit(solution)/shard_map/mul | solution.py:62
  80.0 0.0 copy-start.3
  80.0 3.7 %all-to-all-start.2 = ((f32[32,8,2880]{2,1,0:T(8,128)}), f32[32,8,2880]{2,1,0:T(8,128)}, u32[]{:S(2)}, u32[]{:S(2)}) async-start(f32[32,8,2880]{2,1,0:T(8,128)} %bitcast.52), calls=%async_computation.2 | async-start | bytes 6029312 | tf_op jit(solution)/shard_map/all_to_all | solution.py:63
  83.7 0.0 all-gather.2.cloned.1.call-start
  83.7 0.7 all-gather.2.cloned.1.call-update
  84.4 0.0 all-reduce.3.cloned.1.call-start
  84.5 67.0 %all-gather.2.cloned.1.call-done = bf16[256,2880]{1,0:T(8,128)(2,1)} async-done(((bf16[8,2880]{1,0:T(8,128)(2,1)}), bf16[256,2880]{1,0:T(8,128)(2,1)}) %all-gather.2.cloned.1.call-update) | async-done | bytes 1474576 | tf_op jit(solution)/shard_map/all_gather | solution.py:38
  151.4 0.0 copy-done
  151.4 0.0 copy-done.3
  151.4 5.8 %fusion.35 = f32[256,2880]{1,0:T(8,128)} fusion(bf16[512,2880]{0,1:T(8,128)(2,1)S(1)} %copy-done, bf16[256,2880]{1,0:T(8,128)(2,1)} %all-gather.2.cloned.1.call-done, bf16[2880,512]{1,0:T(8,128)(2,1)} %param.16, f32[512]{0:T(512)S(1)} %copy-done.3), kind=kOutput, calls=%fused_computation.21 | convolution fusion | flops 1510342656 | bytes 10323968 | tf_op jit(solution)/shard_map/dot_general | solution.py:70
  157.3 0.0 all-reduce.3.cloned.1.call-update
  157.3 0.0 copy-start.2
  157.3 0.1 reshape.97
  157.4 0.1 reshape_reshape.2
  157.5 1.7 all-to-all-done.2
  159.3 6.2 %scatter_custom_fusion.2 = f32[8,2880]{1,0:T(8,128)S(1)} fusion(s32[256]{0:T(256)S(1)} %bitcast.55, f32[32,8,2880]{2,1,0:T(8,128)} %all-to-all-done.2, f32[]{:T(128)} %constant.46.clone.1), kind=kCustom, calls=%fused_computation.5 | custom fusion | flops 737280 | bytes 3041284 | tf_op jit(solution)/shard_map/scatter-add | solution.py:67
  165.4 128.8 %all-reduce.3.cloned.1.call-done = f32[256,2880]{1,0:T(8,128)} async-done(((f32[256,2880]{1,0:T(8,128)}), f32[256,2880]{1,0:T(8,128)}) %all-reduce.3.cloned.1.call-update) | async-done | bytes 2949136
  294.2 0.0 copy-done.2
  294.2 1.5 fusion.46
  (8 shorter events, 0.0 us)
Async XLA Ops:
  6.5 144.9 %copy-start = (bf16[512,2880]{0,1:T(8,128)(2,1)S(1)}, bf16[512,2880]{0,1:T(8,128)(2,1)}, u32[]{:S(2)}) copy-start(bf16[512,2880]{0,1:T(8,128)(2,1)} %param.18) | copy-start | bytes 8847364
  6.5 12.7 %copy-start.1 = (bf16[8,2880]{1,0:T(8,128)(2,1)S(1)}, bf16[8,2880]{1,0:T(8,128)(2,1)}, u32[]{:S(2)}) copy-start(bf16[8,2880]{1,0:T(8,128)(2,1)} %param.10) | copy-start | bytes 138244
  11.1 14.4 %all-to-all-start.1 = ((bf16[32,8,1]{1,2,0:T(2,128)(2,1)}), bf16[32,8,1]{1,2,0:T(2,128)(2,1)S(1)}, u32[]{:S(2)}, u32[]{:S(2)}) async-start(bf16[32,8,1]{1,2,0:T(2,128)(2,1)} %copy.26), calls=%async_computation.1 | async-start | bytes 32768 | tf_op jit(solution)/shard_map/all_to_all | solution.py:51
  26.7 39.9 %all-to-all-start = ((bf16[32,8,2880]{2,1,0:T(8,128)(2,1)}), bf16[32,8,2880]{2,1,0:T(8,128)(2,1)}, u32[]{:S(2)}, u32[]{:S(2)}) async-start(bf16[32,8,2880]{2,1,0:T(8,128)(2,1)} %bitcast.53), calls=%async_computation | async-start | bytes 3014656 | tf_op jit(solution)/shard_map/all_to_all | solution.py:48
  80.0 71.4 %copy-start.3 = (f32[512]{0:T(512)S(1)}, f32[512]{0:T(512)}, u32[]{:S(2)}) copy-start(f32[512]{0:T(512)} %param.17) | copy-start | bytes 6148
  80.0 79.3 %all-to-all-start.2 = ((f32[32,8,2880]{2,1,0:T(8,128)}), f32[32,8,2880]{2,1,0:T(8,128)}, u32[]{:S(2)}, u32[]{:S(2)}) async-start(f32[32,8,2880]{2,1,0:T(8,128)} %bitcast.52), calls=%async_computation.2 | async-start | bytes 6029312 | tf_op jit(solution)/shard_map/all_to_all | solution.py:63
  83.7 67.7 %all-gather.2.cloned.1.call-start = ((), (), s32[]{:S(2)}) async-start(), calls=%async_computation.3 | async-start | bytes 1554432 | tf_op jit(solution)/shard_map/all_gather | solution.py:38
  84.4 209.8 %all-reduce.3.cloned.1.call-start = ((), (), s32[]{:S(2)}) async-start(), calls=%async_computation.4 | async-start | bytes 6029312
  157.3 136.9 %copy-start.2 = (f32[2880]{0:T(1024)S(1)}, f32[2880]{0:T(1024)}, u32[]{:S(2)}) copy-start(f32[2880]{0:T(1024)} %param.19) | copy-start | bytes 34564
Sparse Core Ops, SparseCore 0:
  87.3 64.0 all-gather.1
  157.4 136.7 all-reduce.2
where the time goes:
time: 303 us
  waiting for transfers between devices  238 us (79%)
  matrix products  15.8 us (5%)
  starting transfers between devices  14.5 us (5%)
  between operations  13.5 us (4%)
  local copies, waits for them, and re-layouts  10.7 us (4%)
  other arithmetic  9.9 us (3%)
    unnamed x3, waiting for transfers between devices  130 us
    all_gather x1, waiting for transfers between devices, shards(): lax.all_gather(tokens, 'expert', axis=0, tiled=True)  67 us
    all_to_all x1, waiting for transfers between devices, shards(): lax.all_to_all(widen(send_rows, experts, SLABS), 'expert', split_axis=0,...  36.3 us
    all_to_all x1, starting transfers between devices, shards(): lax.all_to_all(widen(slot_gate, experts, SLABS), 'expert', split_axis=0,...  7.3 us
    dot_general x1, matrix products, shards(): partial_out = jnp.dot(hidden, w_down[0], preferred_element_type=jnp.float32)  7.13 us
    scatter-add x1, other arithmetic, shards(): jnp.zeros((tok_dev, tokens.shape[1]), jnp.float32).at[back_token]  6.17 us
  transfers between devices with their start and end apart: 5, of which 5 were waited for; matrix products, arithmetic and copies ran while one was open for 5% of the time, Pallas kernels for 0%

commit v1 on v0

v1 whole, which is shorter than its diff:
```python
import functools

import jax
import jax.numpy as jnp
from jax import lax
from jax.experimental import pallas as pl
from jax.experimental.pallas import tpu as pltpu
from jax.sharding import PartitionSpec as P

SLABS = 4
LANES = 128
F32 = jnp.float32
BF16 = jnp.bfloat16


def cut(width, parts):
    tiles = -(-width // LANES)
    edges = [LANES * (tiles * i // parts) for i in range(parts)] + [width]
    return list(zip(edges[:-1], edges[1:]))


class Plan:
    def __init__(self, n, d):
        self.n, self.d = n, d
        self.bits = n.bit_length() - 1
        self.half = n // 2
        self.rows = 8 * n
        self.wide = -(-(d + n // SLABS) // LANES) * LANES
        tiles = self.wide // LANES
        self.left = LANES * (tiles // 2)
        self.right = self.wide - self.left
        self.chunks = cut(d, 2)
        low = list(range(self.bits - 2, 0, -1))
        swapped = low[:-2] + low[-2:][::-1]
        self.orders = [low + [0], swapped + [0]]

    def weight(self, j):
        return 2 ** (self.bits - 2 - j)

    def split(self, done):
        run, rest = 1, list(done)
        j = self.bits - 2
        while j in rest:
            rest.remove(j)
            run *= 2
            j -= 1
        offsets = [0]
        for j in rest:
            offsets = offsets + [o + self.weight(j) for o in offsets]
        return run, rest, sorted(offsets)


def body(plan, tokens, routes, gates, w_gate, w_up, w_down, w_enc, b_enc, w_dec, b_dec, out, *scratch):
    p = plan
    chunks = len(p.chunks)
    (v_gate, v_up, v_down, v_enc, v_dec, flat, fold, fold_in, x_left, x_right, hid, feat) = scratch[:12]
    rest = list(scratch[12:])
    acc = [rest.pop(0) for _ in range(chunks)]
    send = [[rest.pop(0) for _ in range(p.bits - 1)] for _ in range(chunks)]
    recv = [[rest.pop(0) for _ in range(p.bits - 1)] for _ in range(chunks)]
    last = [rest.pop(0) for _ in range(chunks)]
    load_sem, ag_send, ag_recv, rs_send, rs_recv = rest

    me = lax.axis_index("expert")
    bit = [(me // 2**j) % 2 for j in range(p.bits)]
    partner = [me + (1 - 2 * bit[j]) * 2**j for j in range(p.bits)]
    top = p.bits - 1

    loads = [
        pltpu.make_async_copy(src, dst, load_sem.at[i])
        for i, (src, dst) in enumerate(
            [
                (w_gate.at[0], v_gate),
                (w_up.at[0], v_up),
                (w_enc, v_enc),
                (w_down.at[0], v_down),
                (w_dec, v_dec),
            ]
        )
    ]
    for load in loads:
        load.start()

    barrier = pltpu.get_barrier_semaphore()
    for j in range(p.bits):
        pl.semaphore_signal(
            barrier, inc=1, device_id={"expert": partner[j]}, device_id_type=pl.DeviceIdType.MESH
        )

    start = p.d // LANES * LANES
    lane = lax.broadcasted_iota(jnp.int32, (8, p.wide - start), 1) - (p.d - start)
    dense = jnp.zeros((8, p.wide - start), F32)
    chosen = routes[...]
    weights = gates[...].astype(F32)
    for k in range(routes.shape[1]):
        dense = dense + jnp.where(lane == chosen[:, k : k + 1], weights[:, k : k + 1], 0.0)
    flat[:, start:] = dense
    flat[:, : p.d] = tokens[...].astype(F32)
    mine = flat[...]
    lead = mine[:, : p.left]
    if p.right > p.left:
        lead = jnp.concatenate([lead, jnp.zeros((8, p.right - p.left), F32)], axis=1)
    fold[...] = jnp.concatenate([lead, mine[:, p.left :]], axis=0).astype(BF16)

    pl.semaphore_wait(barrier, p.bits)

    count = [0]

    def copy(src, dst, to, sems):
        i = count[0]
        count[0] += 1
        return pltpu.make_async_remote_copy(
            src_ref=src,
            dst_ref=dst,
            send_sem=sems[0].at[i],
            recv_sem=sems[1].at[i],
            device_id={"expert": to},
            device_id_type=pl.DeviceIdType.MESH,
        )

    sent = []
    first = copy(fold, fold_in, partner[top], (ag_send, ag_recv))
    first.start()
    sent.append(first)

    def base(fixed):
        total = 0
        for j in fixed:
            total = total + bit[j] * p.weight(j)
        return total

    low_bits = list(range(p.bits - 1))
    block = pl.multiple_of(base(low_bits) * 16, 16)
    first.wait_recv()
    other = fold_in[...].astype(F32)
    for half, x in ((0, x_left), (1, x_right)):
        width = x.shape[1]
        a = mine[:, : p.left] if half == 0 else mine[:, p.left :]
        b = other[8 * half : 8 * half + 8, :width]
        low = jnp.where(bit[top] == 0, a, b)
        high = jnp.where(bit[top] == 0, b, a)
        x[pl.ds(block, 16), :] = jnp.concatenate([low, high], axis=0).astype(BF16)

    pending = [[], []]
    for s in range(p.bits - 1):
        for half, x in ((0, x_left), (1, x_right)):
            for c in pending[half]:
                c.wait_recv()
            done = p.orders[half][:s]
            j = p.orders[half][s]
            run, extra, offsets = p.split(done)
            fixed = [b for b in low_bits if b not in done]
            origin = base(fixed)
            pending[half] = []
            for o in offsets:
                rows = pl.ds(pl.multiple_of((origin + o) * 16, 16), 16 * run)
                c = copy(x.at[rows], x.at[rows], partner[j], (ag_send, ag_recv))
                c.start()
                sent.append(c)
                pending[half].append(c)
    for half in (0, 1):
        for c in pending[half]:
            c.wait_recv()

    def project(w, cols=None):
        left, right = x_left[...], x_right[:, : p.d - p.left]
        return jnp.dot(left, w[: p.left, :], preferred_element_type=F32) + jnp.dot(
            right, w[p.left :, :], preferred_element_type=F32
        )

    loads[0].wait()
    gate_pre = project(v_gate)
    loads[1].wait()
    up_pre = project(v_up)
    hid[...] = ((up_pre + 1.0) * gate_pre * jax.nn.sigmoid(1.702 * gate_pre)).astype(BF16)
    loads[2].wait()
    feat[...] = jnp.maximum(project(v_enc) + b_enc[...], 0.0).astype(BF16)

    tail = x_right[:, start - p.left :].astype(F32)
    lane = lax.broadcasted_iota(jnp.int32, tail.shape, 1) - (p.d - start)
    scale = jnp.sum(jnp.where(lane == me // SLABS, tail, 0.0), axis=1, keepdims=True)

    count[0] = 0
    flights = [None] * chunks

    def pieces(c, s, own):
        order = p.orders[c % 2][::-1]
        j = order[s]
        fixed = order[: s + 1]
        run, extra, offsets = p.split([b for b in low_bits if b not in fixed])
        origin = base(order[:s]) + (bit[j] if own else 1 - bit[j]) * p.weight(j)
        return [pl.ds(pl.multiple_of((origin + o) * 16, 16), 16 * run) for o in offsets]

    def send_stage(c, s):
        if s < p.bits - 1:
            at = 0
            for rows in pieces(c, s, False):
                send[c][s][at : at + rows.size, :] = acc[c][rows, :].astype(BF16)
                at += rows.size
            to = partner[p.orders[c % 2][::-1][s]]
            flights[c] = copy(send[c][s], recv[c][s], to, (rs_send, rs_recv))
        else:
            rows = pl.ds(pl.multiple_of(block + 8 * (1 - bit[top]), 8), 8)
            flights[c] = copy(acc[c].at[rows], last[c], partner[top], (rs_send, rs_recv))
        flights[c].start()
        sent.append(flights[c])

    loads[3].wait()
    loads[4].wait()
    for c, (lo, hi) in enumerate(p.chunks):
        acc[c][...] = scale * jnp.dot(
            hid[...], v_down[:, lo:hi], preferred_element_type=F32
        ) - jnp.dot(feat[...], v_dec[:, lo:hi], preferred_element_type=F32)
        send_stage(c, 0)
    for s in range(p.bits - 1):
        for c in range(chunks):
            flights[c].wait_recv()
            at = 0
            for rows in pieces(c, s, True):
                acc[c][rows, :] = acc[c][rows, :] + recv[c][s][at : at + rows.size, :].astype(F32)
                at += rows.size
            send_stage(c, s + 1)
    rows = pl.ds(pl.multiple_of(block + 8 * bit[top], 8), 8)
    for c, (lo, hi) in enumerate(p.chunks):
        flights[c].wait_recv()
        out[:, lo:hi] = (acc[c][rows, :] + last[c][...] - b_dec[:, lo:hi]).astype(BF16)
    for c in sent:
        c.wait_send()


def shards(tokens, routes, gates, w_gate, w_up, w_down, w_enc, b_enc, w_dec, b_dec):
    n = lax.axis_size("expert")
    d = tokens.shape[1]
    p = Plan(n, d)
    widths = [hi - lo for lo, hi in p.chunks]
    stage_rows = [p.rows // 2 ** (s + 1) for s in range(p.bits - 1)]
    ag = 1 + sum(len(p.split(o[:s])[2]) for o in p.orders for s in range(p.bits - 1))
    rs = len(widths) * p.bits
    vmem = pl.BlockSpec(memory_space=pltpu.VMEM)
    hbm = pl.BlockSpec(memory_space=pl.ANY)
    scratch = [
        pltpu.VMEM(w_gate.shape[1:], BF16),
        pltpu.VMEM(w_up.shape[1:], BF16),
        pltpu.VMEM(w_down.shape[1:], BF16),
        pltpu.VMEM(w_enc.shape, BF16),
        pltpu.VMEM(w_dec.shape, BF16),
        pltpu.VMEM((8, p.wide), F32),
        pltpu.VMEM((16, p.right), BF16),
        pltpu.VMEM((16, p.right), BF16),
        pltpu.VMEM((p.rows, p.left), BF16),
        pltpu.VMEM((p.rows, p.right), BF16),
        pltpu.VMEM((p.rows, w_gate.shape[2]), BF16),
        pltpu.VMEM((p.rows, w_enc.shape[1]), BF16),
    ]
    scratch += [pltpu.VMEM((p.rows, w), F32) for w in widths]
    scratch += [pltpu.VMEM((r, w), BF16) for w in widths for r in stage_rows] * 2
    scratch += [pltpu.VMEM((8, w), F32) for w in widths]
    scratch += [pltpu.SemaphoreType.DMA((k,)) for k in (5, ag, ag, rs, rs)]
    flops = 2 * p.rows * d * (3 * w_gate.shape[2] + 2 * w_enc.shape[1])
    size = 2 * d * (3 * w_gate.shape[2] + 2 * w_enc.shape[1])
    return pl.pallas_call(
        functools.partial(body, p),
        out_shape=jax.ShapeDtypeStruct(tokens.shape, BF16),
        in_specs=[vmem, vmem, vmem, hbm, hbm, hbm, hbm, vmem, hbm, vmem],
        out_specs=vmem,
        scratch_shapes=scratch,
        cost_estimate=pl.CostEstimate(flops=flops, bytes_accessed=size, transcendentals=0),
        compiler_params=pltpu.CompilerParams(
            collective_id=0, has_side_effects=True, vmem_limit_bytes=56 * 2**20
        ),
    )(
        tokens,
        routes,
        gates,
        w_gate,
        w_up,
        w_down,
        w_enc,
        b_enc.reshape(1, -1),
        w_dec,
        b_dec.reshape(1, -1),
    )


def solution(mesh):
    in_specs = (
        P(("group", "expert"), None),
        P(("group", "expert"), None),
        P(("group", "expert"), None),
        P("expert", None, None),
        P("expert", None, None),
        P("expert", None, None),
        P(None, "expert"),
        P("expert"),
        P("expert", None),
        P(),
    )
    out_specs = P(("group", "expert"), None)
    return jax.shard_map(shards, mesh=mesh, in_specs=in_specs, out_specs=out_specs, check_vma=False)
```

time: 303 us -> 64 us (0.21)
  waiting for transfers between devices: 238 us -> 0 us
  Pallas kernels: 0 us -> 46.8 us
  matrix products: 15.8 us -> 0 us
  starting transfers between devices: 14.5 us -> 0 us
  between operations: 13.5 us -> 0.01 us
  other arithmetic: 9.9 us -> 0 us
  local copies, waits for them, and re-layouts: 10.7 us -> 16.8 us
    unnamed x3 -> x0, waiting for transfers between devices: 130 us -> none
    all_gather x1 -> x0, waiting for transfers between devices: 67 us -> none  [shards(): lax.all_gather(tokens, 'expert', axis=0, tiled=True)]
    pallas_call x0 -> x1, Pallas kernels: none -> 46.8 us  [shards(): pl.pallas_call(functools.partial(body, p), out_shape=jax.ShapeDtypeStruct...]
    all_to_all x3 -> x0, waiting for transfers between devices: 41.7 us -> none  [the longest x1 36.3 us: shards(): lax.all_to_all(widen(send_rows, experts, SLABS), 'expert', split_axis=0,...]
    dot_general x3 -> x0, matrix products: 15.8 us -> none  [the longest x1 7.13 us: shards(): partial_out = jnp.dot(hidden, w_down[0], preferred_element_type=jnp.float32)]
    all_to_all x3 -> x0, starting transfers between devices: 14.4 us -> none  [the longest x1 7.3 us: shards(): lax.all_to_all(widen(slot_gate, experts, SLABS), 'expert', split_axis=0,...]
    unnamed x10 -> x8, local copies, waits for them, and re-layouts: 1.71 us -> 15.5 us
    scatter-add x1 -> x0, other arithmetic: 6.17 us -> none  [shards(): jnp.zeros((tok_dev, tokens.shape[1]), jnp.float32).at[back_token]]
  transfers between devices with their start and end apart: 5 -> 0, of which waited for: 5 -> 0; matrix products, arithmetic and copies ran while one was open for 5% -> 0% of each run, Pallas kernels for 0% -> 0%
where the time goes in v1:
time: 64 us; the launch traced here: 63.6 us
  Pallas kernels  46.8 us (73%)
  local copies, waits for them, and re-layouts  16.8 us (26%)
    pallas_call x1, Pallas kernels, shards(): pl.pallas_call(functools.partial(body, p), out_shape=jax.ShapeDtypeStruct...  46.8 us
    unnamed x8, local copies, waits for them, and re-layouts  15.5 us
    reshape x1, local copies, waits for them, and re-layouts, shards(): b_dec.reshape(1, -1)  1.31 us

profile of v1, /device:TPU:0, one launch (start us, length us, event | category | flops | bytes accessed | tf_op | source)
XLA Modules:
  0.0 63.6 jit_solution(1496356352921757267)
XLA Ops:
  0.0 1.3 %copy.12.gates = bf16[8,4]{1,0:T(8,128)(2,1)} copy(bf16[8,4]{0,1:T(4,128)(2,1)} %param.12) | data formatting | bytes 128 | tf_op args[2]
  1.3 1.3 %copy.11.routes = s32[8,4]{1,0:T(8,128)} copy(s32[8,4]{0,1:T(4,128)} %param.11) | data formatting | bytes 256 | tf_op args[1]
  2.7 1.3 %reshape.7.b_dec = f32[1,2880]{1,0:T(1,128)} reshape(f32[2880]{0:T(1024)} %param.19) | data formatting | bytes 23040 | tf_op jit(solution)/shard_map/reshape | solution.py:281
  4.0 4.1 %copy.13.w_gate = bf16[1,2880,360]{2,1,0:T(8,128)(2,1)} copy(bf16[1,2880,360]{1,2,0:T(8,128)(2,1)} %param.13) | data formatting | bytes 4147200 | tf_op args[3]
  8.1 0.0 copy-start
  8.1 4.3 %copy.14.w_up = bf16[1,2880,360]{2,1,0:T(8,128)(2,1)} copy(bf16[1,2880,360]{1,2,0:T(8,128)(2,1)} %param.14) | data formatting | bytes 4147200 | tf_op args[4]
  12.4 0.0 copy-done
  12.4 3.0 %copy.15.w_dec = bf16[512,2880]{1,0:T(8,128)(2,1)} copy(bf16[512,2880]{0,1:T(8,128)(2,1)S(1)} %copy-done) | data formatting | bytes 5898240 | tf_op args[8]
  15.4 46.8 %shard_map.100 = bf16[8,2880]{1,0:T(8,128)(2,1)} custom-call(bf16[8,2880]{1,0:T(8,128)(2,1)} %tokens.1, s32[8,4]{1,0:T(8,128)} %copy.11.routes, bf16[8,4]{1,0:T(8,128)(2,1)} %copy.12.gates, bf16[1,2880,360]{2,1,0:T(8,128)(2,1)} %copy.13.w_gate, bf16[1,2880,360]{2,1,0:T(8,128)(2,1)} %copy.14.w_up, bf16[1,360,2880]{2,1,0:T(8,128)(2,1)} %w_down.1, ...), custom_call_target="tpu_custom_call" | custom-call | flops 3102474240 | bytes 12119040 | tf_op jit(solution)/shard_map/pallas_call | solution.py:261
  62.2 1.4 %copy.17 = bf16[8,2880]{1,0:T(8,128)(2,1)} copy(bf16[8,2880]{1,0:T(8,128)(2,1)} %shard_map.100) | data formatting | bytes 92160
Async XLA Ops:
  8.1 4.3 %copy-start = (bf16[512,2880]{0,1:T(8,128)(2,1)S(1)}, bf16[512,2880]{0,1:T(8,128)(2,1)}, u32[]{:S(2)}) copy-start(bf16[512,2880]{0,1:T(8,128)(2,1)} %param.18) | copy-start | bytes 8847364

commit v2 on v1

--- a/solution.py
+++ b/solution.py
@@ -50,7 +50,7 @@
         return run, rest, sorted(offsets)
 
 
-def body(plan, tokens, routes, gates, w_gate, w_up, w_down, w_enc, b_enc, w_dec, b_dec, out, *scratch):
+def body(plan, tokens, routes, gates, w_gate, w_up, w_down, w_enc, b_enc, w_dec, out, *scratch):
     p = plan
     chunks = len(p.chunks)
     (v_gate, v_up, v_down, v_enc, v_dec, flat, fold, fold_in, x_left, x_right, hid, feat) = scratch[:12]
@@ -90,10 +90,17 @@
     start = p.d // LANES * LANES
     lane = lax.broadcasted_iota(jnp.int32, (8, p.wide - start), 1) - (p.d - start)
     dense = jnp.zeros((8, p.wide - start), F32)
-    chosen = routes[...]
+    eye = lax.broadcasted_iota(jnp.int32, (8, 8), 0) == lax.broadcasted_iota(jnp.int32, (8, 8), 1)
+
+    def column(row):
+        return jnp.sum(jnp.where(eye, row, 0.0), axis=1, keepdims=True)
+
+    chosen = routes[...].astype(F32)
     weights = gates[...].astype(F32)
-    for k in range(routes.shape[1]):
-        dense = dense + jnp.where(lane == chosen[:, k : k + 1], weights[:, k : k + 1], 0.0)
+    for k in range(routes.shape[0]):
+        dense = dense + jnp.where(
+            lane.astype(F32) == column(chosen[k : k + 1, :]), column(weights[k : k + 1, :]), 0.0
+        )
     flat[:, start:] = dense
     flat[:, : p.d] = tokens[...].astype(F32)
     mine = flat[...]
@@ -162,16 +169,23 @@
         for c in pending[half]:
             c.wait_recv()
 
-    def project(w, cols=None):
+    def by_rows(a, b):
+        return lax.dot_general(a, b, (((1,), (1,)), ((), ())), preferred_element_type=F32)
+
+    def project_rows(w):
+        left, right = x_left[...], x_right[:, : p.d - p.left]
+        return by_rows(left, w[:, : p.left]) + by_rows(right, w[:, p.left :])
+
+    def project(w):
         left, right = x_left[...], x_right[:, : p.d - p.left]
         return jnp.dot(left, w[: p.left, :], preferred_element_type=F32) + jnp.dot(
             right, w[p.left :, :], preferred_element_type=F32
         )
 
     loads[0].wait()
-    gate_pre = project(v_gate)
+    gate_pre = project_rows(v_gate)
     loads[1].wait()
-    up_pre = project(v_up)
+    up_pre = project_rows(v_up)
     hid[...] = ((up_pre + 1.0) * gate_pre * jax.nn.sigmoid(1.702 * gate_pre)).astype(BF16)
     loads[2].wait()
     feat[...] = jnp.maximum(project(v_enc) + b_enc[...], 0.0).astype(BF16)
@@ -210,7 +224,7 @@
     for c, (lo, hi) in enumerate(p.chunks):
         acc[c][...] = scale * jnp.dot(
             hid[...], v_down[:, lo:hi], preferred_element_type=F32
-        ) - jnp.dot(feat[...], v_dec[:, lo:hi], preferred_element_type=F32)
+        ) - by_rows(feat[...], v_dec[lo:hi, :])
         send_stage(c, 0)
     for s in range(p.bits - 1):
         for c in range(chunks):
@@ -223,7 +237,7 @@
     rows = pl.ds(pl.multiple_of(block + 8 * bit[top], 8), 8)
     for c, (lo, hi) in enumerate(p.chunks):
         flights[c].wait_recv()
-        out[:, lo:hi] = (acc[c][rows, :] + last[c][...] - b_dec[:, lo:hi]).astype(BF16)
+        out[:, lo:hi] = acc[c][rows, :] + last[c][...]
     for c in sent:
         c.wait_send()
 
@@ -239,11 +253,11 @@
     vmem = pl.BlockSpec(memory_space=pltpu.VMEM)
     hbm = pl.BlockSpec(memory_space=pl.ANY)
     scratch = [
-        pltpu.VMEM(w_gate.shape[1:], BF16),
-        pltpu.VMEM(w_up.shape[1:], BF16),
+        pltpu.VMEM(w_gate.shape[:0:-1], BF16),
+        pltpu.VMEM(w_up.shape[:0:-1], BF16),
         pltpu.VMEM(w_down.shape[1:], BF16),
         pltpu.VMEM(w_enc.shape, BF16),
-        pltpu.VMEM(w_dec.shape, BF16),
+        pltpu.VMEM(w_dec.shape[::-1], BF16),
         pltpu.VMEM((8, p.wide), F32),
         pltpu.VMEM((16, p.right), BF16),
         pltpu.VMEM((16, p.right), BF16),
@@ -258,10 +272,10 @@
     scratch += [pltpu.SemaphoreType.DMA((k,)) for k in (5, ag, ag, rs, rs)]
     flops = 2 * p.rows * d * (3 * w_gate.shape[2] + 2 * w_enc.shape[1])
     size = 2 * d * (3 * w_gate.shape[2] + 2 * w_enc.shape[1])
-    return pl.pallas_call(
+    total = pl.pallas_call(
         functools.partial(body, p),
-        out_shape=jax.ShapeDtypeStruct(tokens.shape, BF16),
-        in_specs=[vmem, vmem, vmem, hbm, hbm, hbm, hbm, vmem, hbm, vmem],
+        out_shape=jax.ShapeDtypeStruct(tokens.shape, F32),
+        in_specs=[vmem, vmem, vmem, hbm, hbm, hbm, hbm, vmem, hbm],
         out_specs=vmem,
         scratch_shapes=scratch,
         cost_estimate=pl.CostEstimate(flops=flops, bytes_accessed=size, transcendentals=0),
@@ -270,16 +284,16 @@
         ),
     )(
         tokens,
-        routes,
-        gates,
-        w_gate,
-        w_up,
+        routes.T,
+        gates.T,
+        w_gate.transpose(0, 2, 1),
+        w_up.transpose(0, 2, 1),
         w_down,
         w_enc,
         b_enc.reshape(1, -1),
-        w_dec,
-        b_dec.reshape(1, -1),
+        w_dec.T,
     )
+    return (total - b_dec).astype(BF16)
 
 
 def solution(mesh):

time: 64 us -> 48.5 us (0.76)
  local copies, waits for them, and re-layouts: 16.8 us -> 0.01 us
  other arithmetic: 0 us -> 1.52 us
    unnamed x8 -> x2, local copies, waits for them, and re-layouts: 15.5 us -> 0.01 us
    convert_element_type x0 -> x1, other arithmetic: none -> 1.52 us  [shards(): return (total - b_dec).astype(BF16)]
    reshape x1 -> x0, local copies, waits for them, and re-layouts: 1.31 us -> none  [shards(): b_dec.reshape(1, -1)]
where the time goes in v2:
time: 48.5 us; the launch traced here: 48.3 us
  Pallas kernels  46.7 us (96%)
  other arithmetic  1.52 us (3%)
    pallas_call x1, Pallas kernels, shards(): pl.pallas_call(functools.partial(body, p), out_shape=jax.ShapeDtypeStruct...  46.7 us
    convert_element_type x1, other arithmetic, shards(): return (total - b_dec).astype(BF16)  1.52 us

profile of v2, /device:TPU:0, one launch (start us, length us, event | category | flops | bytes accessed | tf_op | source)
XLA Modules:
  0.0 48.3 jit_solution(6704570983393960135)
XLA Ops:
  0.0 0.0 copy-start
  0.0 46.7 %shard_map.100 = f32[8,2880]{1,0:T(8,128)} custom-call(bf16[8,2880]{1,0:T(8,128)(2,1)} %tokens.1, s32[4,8]{1,0:T(4,128)} %bitcast.9, bf16[4,8]{1,0:T(4,128)(2,1)} %bitcast.11, bf16[1,360,2880]{2,1,0:T(8,128)(2,1)} %bitcast.7, bf16[1,360,2880]{2,1,0:T(8,128)(2,1)} %bitcast.8, bf16[1,360,2880]{2,1,0:T(8,128)(2,1)} %w_down.1, bf16[2880,512]{1,0:T(8,128)(2,1)} %w_enc.1, ...), custom_call_target="tpu_custom_call" | custom-call | flops 3102474240 | bytes 12119040 | tf_op jit(solution)/shard_map/pallas_call | solution.py:275
  46.7 0.0 copy-done
  46.8 1.5 %subtract_convert_fusion = bf16[8,2880]{1,0:T(8,128)(2,1)} fusion(f32[8,2880]{1,0:T(8,128)} %shard_map.100, f32[2880]{0:T(1024)S(1)} %copy-done), kind=kLoop, calls=%fused_computation | loop fusion | flops 46080 | bytes 149760 | tf_op jit(solution)/shard_map/convert_element_type | solution.py:296
Async XLA Ops:
  0.0 46.7 %copy-start = (f32[2880]{0:T(1024)S(1)}, f32[2880]{0:T(1024)}, u32[]{:S(2)}) copy-start(f32[2880]{0:T(1024)} %param.19) | copy-start | bytes 34564

commit v3 on v2

--- a/solution.py
+++ b/solution.py
@@ -8,6 +8,8 @@
 from jax.sharding import PartitionSpec as P
 
 SLABS = 4
+PAIRS = 2
+CHUNKS = 4
 LANES = 128
 F32 = jnp.float32
 BF16 = jnp.bfloat16
@@ -26,10 +28,9 @@
         self.half = n // 2
         self.rows = 8 * n
         self.wide = -(-(d + n // SLABS) // LANES) * LANES
-        tiles = self.wide // LANES
-        self.left = LANES * (tiles // 2)
-        self.right = self.wide - self.left
-        self.chunks = cut(d, 2)
+        self.parts = cut(self.wide, 2 * PAIRS)
+        self.fold = max(hi - lo for lo, hi in self.parts)
+        self.chunks = cut(d, CHUNKS)
         low = list(range(self.bits - 2, 0, -1))
         swapped = low[:-2] + low[-2:][::-1]
         self.orders = [low + [0], swapped + [0]]
@@ -53,8 +54,9 @@
 def body(plan, tokens, routes, gates, w_gate, w_up, w_down, w_enc, b_enc, w_dec, out, *scratch):
     p = plan
     chunks = len(p.chunks)
-    (v_gate, v_up, v_down, v_enc, v_dec, flat, fold, fold_in, x_left, x_right, hid, feat) = scratch[:12]
-    rest = list(scratch[12:])
+    (v_gate, v_up, v_down, v_enc, v_dec, flat, fold, fold_in, hid, feat, sum_gate, sum_up, sum_enc) = scratch[:13]
+    rest = list(scratch[13:])
+    x = [rest.pop(0) for _ in p.parts]
     acc = [rest.pop(0) for _ in range(chunks)]
     send = [[rest.pop(0) for _ in range(p.bits - 1)] for _ in range(chunks)]
     recv = [[rest.pop(0) for _ in range(p.bits - 1)] for _ in range(chunks)]
@@ -104,10 +106,18 @@
     flat[:, start:] = dense
     flat[:, : p.d] = tokens[...].astype(F32)
     mine = flat[...]
-    lead = mine[:, : p.left]
-    if p.right > p.left:
-        lead = jnp.concatenate([lead, jnp.zeros((8, p.right - p.left), F32)], axis=1)
-    fold[...] = jnp.concatenate([lead, mine[:, p.left :]], axis=0).astype(BF16)
+
+    def part(c):
+        lo, hi = p.parts[c]
+        return mine[:, lo:hi]
+
+    def padded(value):
+        short = p.fold - value.shape[1]
+        return jnp.concatenate([value, jnp.zeros((8, short), F32)], axis=1) if short else value
+
+    for q in range(PAIRS):
+        both = [padded(part(2 * q)), padded(part(2 * q + 1))]
+        fold[q] = jnp.concatenate(both, axis=0).astype(BF16)
 
     pl.semaphore_wait(barrier, p.bits)
 
@@ -126,9 +136,10 @@
         )
 
     sent = []
-    first = copy(fold, fold_in, partner[top], (ag_send, ag_recv))
-    first.start()
-    sent.append(first)
+    first = [copy(fold.at[q], fold_in.at[q], partner[top], (ag_send, ag_recv)) for q in range(PAIRS)]
+    for c in first:
+        c.start()
+        sent.append(c)
 
     def base(fixed):
         total = 0
@@ -138,59 +149,61 @@
 
     low_bits = list(range(p.bits - 1))
     block = pl.multiple_of(base(low_bits) * 16, 16)
-    first.wait_recv()
-    other = fold_in[...].astype(F32)
-    for half, x in ((0, x_left), (1, x_right)):
-        width = x.shape[1]
-        a = mine[:, : p.left] if half == 0 else mine[:, p.left :]
-        b = other[8 * half : 8 * half + 8, :width]
-        low = jnp.where(bit[top] == 0, a, b)
-        high = jnp.where(bit[top] == 0, b, a)
-        x[pl.ds(block, 16), :] = jnp.concatenate([low, high], axis=0).astype(BF16)
-
-    pending = [[], []]
-    for s in range(p.bits - 1):
-        for half, x in ((0, x_left), (1, x_right)):
-            for c in pending[half]:
-                c.wait_recv()
-            done = p.orders[half][:s]
-            j = p.orders[half][s]
-            run, extra, offsets = p.split(done)
-            fixed = [b for b in low_bits if b not in done]
-            origin = base(fixed)
-            pending[half] = []
-            for o in offsets:
-                rows = pl.ds(pl.multiple_of((origin + o) * 16, 16), 16 * run)
-                c = copy(x.at[rows], x.at[rows], partner[j], (ag_send, ag_recv))
-                c.start()
-                sent.append(c)
-                pending[half].append(c)
-    for half in (0, 1):
-        for c in pending[half]:
-            c.wait_recv()
+    pending = [[] for _ in p.parts]
+
+    def gather_stage(c, s):
+        order = p.orders[c % 2]
+        done, j = order[:s], order[s]
+        run, extra, offsets = p.split(done)
+        origin = base([b for b in low_bits if b not in done])
+        pending[c] = []
+        for o in offsets:
+            rows = pl.ds(pl.multiple_of((origin + o) * 16, 16), 16 * run)
+            flight = copy(x[c].at[rows], x[c].at[rows], partner[j], (ag_send, ag_recv))
+            flight.start()
+            sent.append(flight)
+            pending[c].append(flight)
+
+    def arrived(c):
+        for flight in pending[c]:
+            flight.wait_recv()
+
+    for q in range(PAIRS):
+        first[q].wait_recv()
+        for half in (0, 1):
+            c = 2 * q + half
+            a = part(c)
+            b = fold_in[q].astype(F32)[8 * half : 8 * half + 8, : a.shape[1]]
+            low = jnp.where(bit[top] == 0, a, b)
+            high = jnp.where(bit[top] == 0, b, a)
+            x[c][pl.ds(block, 16), :] = jnp.concatenate([low, high], axis=0).astype(BF16)
+            gather_stage(c, 0)
+    for s in range(1, p.bits - 1):
+        for c in range(len(p.parts)):
+            arrived(c)
+            gather_stage(c, s)
 
     def by_rows(a, b):
         return lax.dot_general(a, b, (((1,), (1,)), ((), ())), preferred_element_type=F32)
 
-    def project_rows(w):
-        left, right = x_left[...], x_right[:, : p.d - p.left]
-        return by_rows(left, w[:, : p.left]) + by_rows(right, w[:, p.left :])
-
-    def project(w):
-        left, right = x_left[...], x_right[:, : p.d - p.left]
-        return jnp.dot(left, w[: p.left, :], preferred_element_type=F32) + jnp.dot(
-            right, w[p.left :, :], preferred_element_type=F32
-        )
-
-    loads[0].wait()
-    gate_pre = project_rows(v_gate)
-    loads[1].wait()
-    up_pre = project_rows(v_up)
-    hid[...] = ((up_pre + 1.0) * gate_pre * jax.nn.sigmoid(1.702 * gate_pre)).astype(BF16)
-    loads[2].wait()
-    feat[...] = jnp.maximum(project(v_enc) + b_enc[...], 0.0).astype(BF16)
-
-    tail = x_right[:, start - p.left :].astype(F32)
+    for load in loads[:3]:
+        load.wait()
+    for c, (lo, hi) in enumerate(p.parts):
+        arrived(c)
+        hi = min(hi, p.d)
+        rows = x[c][:, : hi - lo]
+        terms = [
+            (sum_gate, by_rows(rows, v_gate[:, lo:hi])),
+            (sum_up, by_rows(rows, v_up[:, lo:hi])),
+            (sum_enc, jnp.dot(rows, v_enc[lo:hi, :], preferred_element_type=F32)),
+        ]
+        for total, term in terms:
+            total[...] = term if c == 0 else total[...] + term
+    gate_pre = sum_gate[...]
+    hid[...] = ((sum_up[...] + 1.0) * gate_pre * jax.nn.sigmoid(1.702 * gate_pre)).astype(BF16)
+    feat[...] = jnp.maximum(sum_enc[...] + b_enc[...], 0.0).astype(BF16)
+
+    tail = x[-1][:, start - p.parts[-1][0] :].astype(F32)
     lane = lax.broadcasted_iota(jnp.int32, tail.shape, 1) - (p.d - start)
     scale = jnp.sum(jnp.where(lane == me // SLABS, tail, 0.0), axis=1, keepdims=True)
 
@@ -248,7 +261,7 @@
     p = Plan(n, d)
     widths = [hi - lo for lo, hi in p.chunks]
     stage_rows = [p.rows // 2 ** (s + 1) for s in range(p.bits - 1)]
-    ag = 1 + sum(len(p.split(o[:s])[2]) for o in p.orders for s in range(p.bits - 1))
+    ag = PAIRS + PAIRS * sum(len(p.split(o[:s])[2]) for o in p.orders for s in range(p.bits - 1))
     rs = len(widths) * p.bits
     vmem = pl.BlockSpec(memory_space=pltpu.VMEM)
     hbm = pl.BlockSpec(memory_space=pl.ANY)
@@ -259,13 +272,15 @@
         pltpu.VMEM(w_enc.shape, BF16),
         pltpu.VMEM(w_dec.shape[::-1], BF16),
         pltpu.VMEM((8, p.wide), F32),
-        pltpu.VMEM((16, p.right), BF16),
-        pltpu.VMEM((16, p.right), BF16),
-        pltpu.VMEM((p.rows, p.left), BF16),
-        pltpu.VMEM((p.rows, p.right), BF16),
+        pltpu.VMEM((PAIRS, 16, p.fold), BF16),
+        pltpu.VMEM((PAIRS, 16, p.fold), BF16),
         pltpu.VMEM((p.rows, w_gate.shape[2]), BF16),
         pltpu.VMEM((p.rows, w_enc.shape[1]), BF16),
+        pltpu.VMEM((p.rows, w_gate.shape[2]), F32),
+        pltpu.VMEM((p.rows, w_gate.shape[2]), F32),
+        pltpu.VMEM((p.rows, w_enc.shape[1]), F32),
     ]
+    scratch += [pltpu.VMEM((p.rows, hi - lo), BF16) for lo, hi in p.parts]
     scratch += [pltpu.VMEM((p.rows, w), F32) for w in widths]
     scratch += [pltpu.VMEM((r, w), BF16) for w in widths for r in stage_rows] * 2
     scratch += [pltpu.VMEM((8, w), F32) for w in widths]

time: 48.5 us -> 44.6 us (0.920)
  Pallas kernels: 46.7 us -> 42.9 us
    pallas_call x1, Pallas kernels: 46.7 us -> 42.9 us  [shards(): pl.pallas_call(functools.partial(body, p), out_shape=jax.ShapeDtypeStruct...]
where the time goes in v3:
time: 44.6 us; the launch traced here: 44.4 us
  Pallas kernels  42.9 us (96%)
  other arithmetic  1.52 us (3%)
    pallas_call x1, Pallas kernels, shards(): pl.pallas_call(functools.partial(body, p), out_shape=jax.ShapeDtypeStruct...  42.9 us
    convert_element_type x1, other arithmetic, shards(): return (total - b_dec).astype(BF16)  1.52 us

profile of v3, /device:TPU:0, one launch (start us, length us, event | category | flops | bytes accessed | tf_op | source)
XLA Modules:
  0.0 44.4 jit_solution(1269183531317286793)
XLA Ops:
  0.0 0.0 copy-start
  0.0 42.9 %shard_map.100 = f32[8,2880]{1,0:T(8,128)} custom-call(bf16[8,2880]{1,0:T(8,128)(2,1)} %tokens.1, s32[4,8]{1,0:T(4,128)} %bitcast.9, bf16[4,8]{1,0:T(4,128)(2,1)} %bitcast.11, bf16[1,360,2880]{2,1,0:T(8,128)(2,1)} %bitcast.7, bf16[1,360,2880]{2,1,0:T(8,128)(2,1)} %bitcast.8, bf16[1,360,2880]{2,1,0:T(8,128)(2,1)} %w_down.1, bf16[2880,512]{1,0:T(8,128)(2,1)} %w_enc.1, ...), custom_call_target="tpu_custom_call" | custom-call | flops 3102474240 | bytes 12119040 | tf_op jit(solution)/shard_map/pallas_call | solution.py:290
  42.9 0.0 copy-done
  42.9 1.5 %subtract_convert_fusion = bf16[8,2880]{1,0:T(8,128)(2,1)} fusion(f32[8,2880]{1,0:T(8,128)} %shard_map.100, f32[2880]{0:T(1024)S(1)} %copy-done), kind=kLoop, calls=%fused_computation | loop fusion | flops 46080 | bytes 149760 | tf_op jit(solution)/shard_map/convert_element_type | solution.py:311
Async XLA Ops:
  0.0 42.9 %copy-start = (f32[2880]{0:T(1024)S(1)}, f32[2880]{0:T(1024)}, u32[]{:S(2)}) copy-start(f32[2880]{0:T(1024)} %param.19) | copy-start | bytes 34564

commit v4 on v3

--- a/solution.py
+++ b/solution.py
@@ -8,8 +8,8 @@
 from jax.sharding import PartitionSpec as P
 
 SLABS = 4
-PAIRS = 2
-CHUNKS = 4
+PAIRS = 3
+CHUNKS = 6
 LANES = 128
 F32 = jnp.float32
 BF16 = jnp.bfloat16
@@ -32,8 +32,11 @@
         self.fold = max(hi - lo for lo, hi in self.parts)
         self.chunks = cut(d, CHUNKS)
         low = list(range(self.bits - 2, 0, -1))
-        swapped = low[:-2] + low[-2:][::-1]
-        self.orders = [low + [0], swapped + [0]]
+        near, turn = low[:-3], low[-3:]
+        self.orders = [near + turn[i:] + turn[:i] + [0] for i in range(len(turn))]
+
+    def order(self, c):
+        return self.orders[c % len(self.orders)]
 
     def weight(self, j):
         return 2 ** (self.bits - 2 - j)
@@ -152,7 +155,7 @@
     pending = [[] for _ in p.parts]
 
     def gather_stage(c, s):
-        order = p.orders[c % 2]
+        order = p.order(c)
         done, j = order[:s], order[s]
         run, extra, offsets = p.split(done)
         origin = base([b for b in low_bits if b not in done])
@@ -211,7 +214,7 @@
     flights = [None] * chunks
 
     def pieces(c, s, own):
-        order = p.orders[c % 2][::-1]
+        order = p.order(c)[::-1]
         j = order[s]
         fixed = order[: s + 1]
         run, extra, offsets = p.split([b for b in low_bits if b not in fixed])
@@ -224,7 +227,7 @@
             for rows in pieces(c, s, False):
                 send[c][s][at : at + rows.size, :] = acc[c][rows, :].astype(BF16)
                 at += rows.size
-            to = partner[p.orders[c % 2][::-1][s]]
+            to = partner[p.order(c)[::-1][s]]
             flights[c] = copy(send[c][s], recv[c][s], to, (rs_send, rs_recv))
         else:
             rows = pl.ds(pl.multiple_of(block + 8 * (1 - bit[top]), 8), 8)
@@ -261,7 +264,9 @@
     p = Plan(n, d)
     widths = [hi - lo for lo, hi in p.chunks]
     stage_rows = [p.rows // 2 ** (s + 1) for s in range(p.bits - 1)]
-    ag = PAIRS + PAIRS * sum(len(p.split(o[:s])[2]) for o in p.orders for s in range(p.bits - 1))
+    ag = PAIRS + sum(
+        len(p.split(p.order(c)[:s])[2]) for c in range(2 * PAIRS) for s in range(p.bits - 1)
+    )
     rs = len(widths) * p.bits
     vmem = pl.BlockSpec(memory_space=pltpu.VMEM)
     hbm = pl.BlockSpec(memory_space=pl.ANY)

time: 44.6 us -> 43.6 us (0.978)
  Pallas kernels: 42.9 us -> 41.9 us
    pallas_call x1, Pallas kernels: 42.9 us -> 41.9 us  [shards(): pl.pallas_call(functools.partial(body, p), out_shape=jax.ShapeDtypeStruct...]
where the time goes in v4:
time: 43.6 us; the launch traced here: 43.4 us
  Pallas kernels  41.9 us (96%)
  other arithmetic  1.52 us (3%)
    pallas_call x1, Pallas kernels, shards(): pl.pallas_call(functools.partial(body, p), out_shape=jax.ShapeDtypeStruct...  41.9 us
    convert_element_type x1, other arithmetic, shards(): return (total - b_dec).astype(BF16)  1.52 us

profile of v4, /device:TPU:0, one launch (start us, length us, event | category | flops | bytes accessed | tf_op | source)
XLA Modules:
  0.0 43.4 jit_solution(3732851707423702976)
XLA Ops:
  0.0 0.0 copy-start
  0.0 41.9 %shard_map.100 = f32[8,2880]{1,0:T(8,128)} custom-call(bf16[8,2880]{1,0:T(8,128)(2,1)} %tokens.1, s32[4,8]{1,0:T(4,128)} %bitcast.9, bf16[4,8]{1,0:T(4,128)(2,1)} %bitcast.11, bf16[1,360,2880]{2,1,0:T(8,128)(2,1)} %bitcast.7, bf16[1,360,2880]{2,1,0:T(8,128)(2,1)} %bitcast.8, bf16[1,360,2880]{2,1,0:T(8,128)(2,1)} %w_down.1, bf16[2880,512]{1,0:T(8,128)(2,1)} %w_enc.1, ...), custom_call_target="tpu_custom_call" | custom-call | flops 3102474240 | bytes 12119040 | tf_op jit(solution)/shard_map/pallas_call | solution.py:295
  41.9 0.0 copy-done
  41.9 1.5 %subtract_convert_fusion = bf16[8,2880]{1,0:T(8,128)(2,1)} fusion(f32[8,2880]{1,0:T(8,128)} %shard_map.100, f32[2880]{0:T(1024)S(1)} %copy-done), kind=kLoop, calls=%fused_computation | loop fusion | flops 46080 | bytes 149760 | tf_op jit(solution)/shard_map/convert_element_type | solution.py:316
Async XLA Ops:
  0.0 41.9 %copy-start = (f32[2880]{0:T(1024)S(1)}, f32[2880]{0:T(1024)}, u32[]{:S(2)}) copy-start(f32[2880]{0:T(1024)} %param.19) | copy-start | bytes 34564
